TPU v7x, 256 devices: a whole 4x4x8 slice. The times are simulated.
256 devices in a mesh: blk: 128 (over x_lo, y, z, core), dp: 2 (over x_hi).
Axes of the slice: x: 4 (x_hi: 2, x_lo: 2; x = x_hi * 2 + x_lo), y: 4, z: 8, core: 2. Of those that a mesh axis runs over, the one named last changes fastest.
Arguments:
- fresh_rows: bfloat16 [131072, 2048], P(('blk', 'dp')), may hold values from -6 to 6
- older_rows: bfloat16 [131072, 2048], P(('blk', 'dp')), may hold values from -6 to 6
- older_cotangent: bfloat16 [131072, 2048], P(('blk', 'dp')), may hold values from -6 to 6
- weight_up: bfloat16 [2048, 5120], P(None, 'blk'), may hold values from -0.125 to 0.125
- weight_down: bfloat16 [5120, 2048], P('blk'), may hold values from -0.3125 to 0.3125
Outputs:
- fresh_output: bfloat16 [131072, 2048], P(('blk', 'dp'))
- older_input_grad: bfloat16 [131072, 2048], P(('blk', 'dp'))
- gradient_up: float32 [2048, 5120], P(None, 'blk')
- gradient_down: float32 [5120, 2048], P('blk')
All inputs are finite; a program needn't handle non-finite values.
Results may differ from a plain program's by a relative error of at most 0.0049.
Values may be sent and summed in bfloat16 or wider, within the bound.
A program may use at most 192 MiB of HBM per device.

v0:
```python
import functools

import jax
import jax.numpy as jnp
from jax import lax
from jax.experimental import pallas as pl
from jax.experimental.pallas import tpu as pltpu
from jax.sharding import PartitionSpec as P

MESH = pl.DeviceIdType.MESH
WINDOW = 8
REACH = WINDOW // 2
SLOTS = 2 * REACH + 1
SEAM = 32
COL_TILE = 512


def contract(left, right, dims):
    return lax.dot_general(left, right, (dims, ((), ())), preferred_element_type=jnp.float32)


def kernel(
    fresh_hbm, older_hbm, cot_hbm, up_ref, down_ref,
    out_hbm, igrad_hbm, grads_hbm,
    w, fresh, older, cot, grads_acc, act_t, gact_t, out_v, igrad_v, grads_v,
    sib_out, sib_in, x_out, x_in, x0_out, x0_in, z_out, z_in, z0_in,
    in_sem, out_sem,
    b_ss, b_rs, f_ss, f_rs, bs_ss, bs_rs, fs_ss, fs_rs,
    g_ss, g_rs, x_ss, x_rs, z_ss, z_rs, d_ss, d_rs,
):
    units, width = up_ref.shape
    packed = 2 * units
    pair = 2 * packed
    half = width // 2
    rows = older.shape[0]
    count = lax.axis_size("blk")
    me = lax.axis_index("blk")
    g = lax.axis_index("dp")
    k = lax.rem(me, 2)
    chip = me // 2
    ahead = lax.rem(me + 2, count)
    behind = lax.rem(me + count - 2, count)
    sibling = me + 1 - 2 * k
    other = 1 - g
    seam_up = lax.rem(chip, SEAM) == SEAM - 1
    seam_down = lax.rem(chip, SEAM) == 0

    barrier = pltpu.get_barrier_semaphore()
    peers = ((ahead, g), (behind, g), (sibling, g), (me, other), (ahead, other), (behind, other))
    for peer in peers:
        pl.semaphore_signal(barrier, inc=1, device_id=peer, device_id_type=MESH)

    loads = [
        pltpu.make_async_copy(src, dst, in_sem.at[i])
        for i, (src, dst) in enumerate(((older_hbm, older), (cot_hbm, cot), (fresh_hbm, fresh)))
    ]
    for load in loads:
        load.start()

    my_rows = pl.multiple_of(k * packed, 16)
    sib_rows = pl.multiple_of((1 - k) * packed, 16)
    my_cols = pl.multiple_of(g * half, 128)
    other_cols = pl.multiple_of(other * half, 128)
    w[REACH, pl.ds(my_rows, packed), :] = jnp.concatenate([up_ref[...], down_ref[...]], axis=0)
    w[0, 0:packed, :] = jnp.zeros((packed, width), w.dtype)
    w[SLOTS - 1, packed:pair, :] = jnp.zeros((packed, width), w.dtype)

    pl.semaphore_wait(barrier, len(peers))

    def remote(src, dst, send, recv, device):
        return pltpu.make_async_remote_copy(
            src_ref=src, dst_ref=dst, send_sem=send, recv_sem=recv,
            device_id=device, device_id_type=MESH,
        )

    def piece(slot, start, q):
        return w.at[slot, pl.ds(start, packed), pl.ds(q * half, half)]

    def send_back(h, q):
        group = jnp.where(seam_down, other, g) if q == 1 else g
        return remote(
            piece(REACH + h, my_rows, q), piece(REACH + h + 1, my_rows, q),
            b_ss.at[h, q], b_rs.at[h + 1, q], (behind, group),
        )

    def send_forth(h, q):
        group = jnp.where(seam_up, other, g) if q == 1 else g
        return remote(
            piece(REACH - h, my_rows, q), piece(REACH - h - 1, my_rows, q),
            f_ss.at[h, q], f_rs.at[h + 1, q], (ahead, group),
        )

    def recv_back(h, q):
        dst = piece(REACH + h, my_rows, q)
        return remote(dst, dst, b_ss.at[h, q], b_rs.at[h, q], (behind, g))

    def recv_forth(h, q):
        dst = piece(REACH - h, my_rows, q)
        return remote(dst, dst, f_ss.at[h, q], f_rs.at[h, q], (ahead, g))

    def share(slot, h, q, start, send, recv):
        ref = piece(slot, start, q)
        return remote(ref, ref, send.at[h, q], recv.at[h, q], (sibling, g))

    def share_back(h, q, start=my_rows):
        return share(REACH + h, h, q, start, bs_ss, bs_rs)

    def share_forth(h, q, start=my_rows):
        return share(REACH - h, h, q, start, fs_ss, fs_rs)

    def share_grads(h):
        return remote(sib_out.at[h], sib_in.at[h], g_ss.at[h], g_rs.at[h], (sibling, g))

    def swap(h):
        return remote(x_out.at[h], x_in.at[h], x_ss.at[h], x_rs.at[h], (me, other))

    def swap_last():
        return remote(x0_out, x0_in, x_ss.at[0], x_rs.at[0], (me, other))

    def carry(h):
        return remote(z_out.at[h], z_in.at[h - 1], z_ss.at[h], z_rs.at[h - 1], (ahead, g))

    def carry_last(cross):
        return remote(
            z_out.at[1], z0_in.at[:, pl.ds(my_cols, half)],
            (d_ss if cross else z_ss).at[1], (d_rs if cross else z_rs).at[0],
            (ahead, other if cross else g),
        )

    for q in range(2):
        share_back(0, q).start()
        send_back(0, q).start()
        send_forth(0, q).start()

    def valid(offset):
        return jnp.logical_and(offset >= 0, offset < WINDOW)

    def compute_back(h):
        block = w[REACH + h]
        pre = contract(block, older[...], ((1,), (1,)))
        through = contract(block, cot[...], ((1,), (1,)))
        blank = jnp.zeros((units, rows), jnp.float32)
        gact, act = [], []
        for p in range(2):
            keep = valid(2 * h + p - k)
            relu = jnp.maximum(pre[p * packed:p * packed + units], 0.0)
            thr = through[p * packed + units:(p + 1) * packed]
            gact += [jnp.where(keep, thr * 2.0 * relu, 0.0), blank]
            act += [blank, jnp.where(keep, jnp.square(relu), 0.0)]
        gact = jnp.concatenate(gact, axis=0).astype(jnp.bfloat16)
        act = jnp.concatenate(act, axis=0).astype(jnp.bfloat16)
        gact_t[h] = gact

        @pl.loop(0, width // COL_TILE)
        def _(t):
            cols = pl.ds(pl.multiple_of(t * COL_TILE, COL_TILE), COL_TILE)
            grads_acc[h, :, cols] = (
                contract(gact_t[h], older[:, cols], ((1,), (0,)))
                + contract(act, cot[:, cols], ((1,), (0,)))
            )

        sib_out[h] = grads_acc[h, pl.ds(sib_rows, packed), :].astype(jnp.bfloat16)

    def reduce_near(h):
        share_grads(h).wait_recv()
        mine = grads_acc.at[h, pl.ds(my_rows, packed)]
        mine[:, pl.ds(my_cols, half)] += sib_in[h, :, pl.ds(my_cols, half)].astype(jnp.float32)
        x_out[h] = (
            mine[:, pl.ds(other_cols, half)]
            + sib_in[h, :, pl.ds(other_cols, half)].astype(jnp.float32)
        ).astype(jnp.bfloat16)
        swap(h).start()

    def reduce_own():
        share_grads(0).wait_recv()
        x0_out[...] = (
            grads_acc[0, pl.ds(my_rows, packed), :] + sib_in[0].astype(jnp.float32)
        ).astype(jnp.bfloat16)
        swap_last().start()

    @pl.loop(0, REACH + 1)
    def _(h):
        @pl.when(h == 0)
        def _():
            loads[0].wait()
            loads[1].wait()

        @pl.when(h > 0)
        def _():
            for q in range(2):
                @pl.when(h <= REACH - k)
                def _():
                    recv_back(h, q).wait_recv()

                    @pl.when(h + 1 <= REACH - k)
                    def _():
                        send_back(h, q).start()

                    share_back(h, q).start()

                @pl.when(h <= REACH - 1 + k)
                def _():
                    recv_forth(h, q).wait_recv()

                    @pl.when(h + 1 <= REACH - 1 + k)
                    def _():
                        send_forth(h, q).start()

                    share_forth(h, q).start()

        @pl.when(h == 1)
        def _():
            reduce_own()

        @pl.when(h > 1)
        def _():
            reduce_near(h - 1)

        @pl.when(h <= REACH - 1 + k)
        def _():
            for q in range(2):
                share_back(h, q, sib_rows).wait_recv()
            compute_back(h)

            share_grads(h).start()

    def chain(h, first):
        swap(h).wait_recv()
        total = (
            grads_acc[h, pl.ds(my_rows, packed), pl.ds(my_cols, half)]
            + x_in[h].astype(jnp.float32)
        )
        if not first:
            carry(h + 1).wait_recv()
            total = total + z_in[h].astype(jnp.float32)
        z_out[h] = total.astype(jnp.bfloat16)
        if h == 1:
            carry_last(False).start()
            carry_last(True).start()
        else:
            carry(h).start()

    @pl.when(k == 0)
    def _():
        share_grads(REACH).wait_recv()
        grads_acc[REACH, 0:packed, pl.ds(my_cols, half)] = (
            sib_in[REACH, :, pl.ds(my_cols, half)].astype(jnp.float32)
        )
        x_out[REACH] = sib_in[REACH, :, pl.ds(other_cols, half)]
        swap(REACH).start()
        gact_t[REACH] = jnp.zeros((pair, rows), jnp.bfloat16)

    @pl.when(k == 1)
    def _():
        chain(REACH - 1, True)

    loads[2].wait()
    for q in range(2):
        pass

    @pl.loop(1, REACH + 1)
    def _(h):
        @pl.when(h <= REACH - k)
        def _():
            for q in range(2):
                share_forth(h, q, sib_rows).wait_recv()

    @pl.loop(0, REACH + 1)
    def _(s):
        pre = contract(w[s], fresh[...], ((1,), (1,)))
        blank = jnp.zeros((units, rows), jnp.float32)
        act = []
        for p in range(2):
            keep = valid(k - 2 * (s - REACH) - p)
            relu = jnp.maximum(pre[p * packed:p * packed + units], 0.0)
            act += [blank, jnp.where(keep, jnp.square(relu), 0.0)]
        act_t[s] = jnp.concatenate(act, axis=0).astype(jnp.bfloat16)

    @pl.when(k == 0)
    def _():
        chain(REACH, True)

    def finish(lhs_ref, first_slot, dst, dst_hbm, sem):
        lhs = lhs_ref[...].reshape((REACH + 1) * pair, rows).T

        @pl.loop(0, width // COL_TILE)
        def _(t):
            cols = pl.ds(pl.multiple_of(t * COL_TILE, COL_TILE), COL_TILE)
            right = w[first_slot:first_slot + REACH + 1, :, cols].reshape((REACH + 1) * pair, COL_TILE)
            dst[:, cols] = contract(lhs, right, ((1,), (0,))).astype(dst.dtype)

        pltpu.make_async_copy(dst, dst_hbm, sem).start()

    finish(act_t, 0, out_v, out_hbm, out_sem.at[0])

    @pl.when(k == 0)
    def _():
        chain(REACH - 1, False)

    finish(gact_t, REACH, igrad_v, igrad_hbm, out_sem.at[1])

    for h in range(REACH - 2, 0, -1):
        chain(h, False)

    swap_last().wait_recv()
    remote(
        z_out.at[1], z0_in.at[:, pl.ds(my_cols, half)], z_ss.at[1], z_rs.at[0], (ahead, g)
    ).wait_recv()
    remote(
        z_out.at[1], z0_in.at[:, pl.ds(other_cols, half)], d_ss.at[1], d_rs.at[0], (ahead, other)
    ).wait_recv()
    total = x0_out[...].astype(jnp.float32) + x0_in[...].astype(jnp.float32)
    grads_v[...] = (total + z0_in[...].astype(jnp.float32)) * (1.0 / rows)
    last = pltpu.make_async_copy(grads_v, grads_hbm, out_sem.at[2])
    last.start()

    for q in range(2):
        share_back(0, q).wait_send()
        send_back(0, q).wait_send()
        send_forth(0, q).wait_send()

    @pl.loop(1, REACH + 1)
    def _(h):
        @pl.when(h <= REACH - k)
        def _():
            for q in range(2):
                @pl.when(h + 1 <= REACH - k)
                def _():
                    send_back(h, q).wait_send()

                share_back(h, q).wait_send()

        @pl.when(h <= REACH - 1 + k)
        def _():
            for q in range(2):
                @pl.when(h + 1 <= REACH - 1 + k)
                def _():
                    send_forth(h, q).wait_send()

                share_forth(h, q).wait_send()

    for h in range(REACH):
        share_grads(h).wait_send()
    swap_last().wait_send()
    for h in range(1, REACH):
        swap(h).wait_send()
    carry_last(False).wait_send()
    carry_last(True).wait_send()
    for h in range(2, REACH):
        carry(h).wait_send()

    @pl.when(k == 1)
    def _():
        share_grads(REACH).wait_send()

    @pl.when(k == 0)
    def _():
        swap(REACH).wait_send()
        carry(REACH).wait_send()

    pltpu.make_async_copy(out_v, out_hbm, out_sem.at[0]).wait()
    pltpu.make_async_copy(igrad_v, igrad_hbm, out_sem.at[1]).wait()
    last.wait()


def per_device(fresh_rows, older_rows, older_cotangent, weight_up, weight_down):
    rows, width = fresh_rows.shape
    units = weight_up.shape[1]
    packed = 2 * units
    pair = 2 * packed
    half = width // 2
    bf16, f32 = jnp.bfloat16, jnp.float32
    hops = REACH + 1
    dma = pltpu.SemaphoreType.DMA
    out, igrad, grads = pl.pallas_call(
        kernel,
        out_shape=(
            jax.ShapeDtypeStruct((rows, width), bf16),
            jax.ShapeDtypeStruct((rows, width), bf16),
            jax.ShapeDtypeStruct((packed, width), f32),
        ),
        in_specs=[pl.BlockSpec(memory_space=pl.ANY)] * 3
        + [pl.BlockSpec(memory_space=pltpu.VMEM)] * 2,
        out_specs=[pl.BlockSpec(memory_space=pl.ANY)] * 3,
        scratch_shapes=[
            pltpu.VMEM((SLOTS, pair, width), bf16),
            pltpu.VMEM((rows, width), bf16),
            pltpu.VMEM((rows, width), bf16),
            pltpu.VMEM((rows, width), bf16),
            pltpu.VMEM((hops, pair, width), f32),
            pltpu.VMEM((hops, pair, rows), bf16),
            pltpu.VMEM((hops, pair, rows), bf16),
            pltpu.VMEM((rows, width), bf16),
            pltpu.VMEM((rows, width), bf16),
            pltpu.VMEM((packed, width), f32),
            pltpu.VMEM((hops, packed, width), bf16),
            pltpu.VMEM((hops, packed, width), bf16),
            pltpu.VMEM((hops, packed, half), bf16),
            pltpu.VMEM((hops, packed, half), bf16),
            pltpu.VMEM((packed, width), bf16),
            pltpu.VMEM((packed, width), bf16),
            pltpu.VMEM((hops, packed, half), bf16),
            pltpu.VMEM((hops, packed, half), bf16),
            pltpu.VMEM((packed, width), bf16),
            dma((3,)), dma((3,)),
        ]
        + [dma((hops, 2))] * 8
        + [dma((hops,))] * 8,
        compiler_params=pltpu.CompilerParams(
            collective_id=0, has_side_effects=True, vmem_limit_bytes=56 * 2**20
        ),
    )(fresh_rows, older_rows, older_cotangent, weight_up.T, weight_down)
    return out, igrad, grads[:units].T, grads[units:]


def solution(mesh):
    in_specs = (
        P(("blk", "dp"), None),
        P(("blk", "dp"), None),
        P(("blk", "dp"), None),
        P(None, "blk"),
        P("blk", None),
    )
    out_specs = (P(("blk", "dp"), None), P(("blk", "dp"), None), P(None, "blk"), P("blk", None))
    return jax.shard_map(
        per_device, mesh=mesh, in_specs=in_specs, out_specs=out_specs, check_vma=False
    )
```

profile of v0, /device:TPU:96, one launch (start us, length us, event | category | flops | bytes accessed | tf_op | source)
XLA Modules:
  0.0 89.1 jit_solution(7002980838279338532)
XLA Ops:
  0.6 81.9 %shard_map.84 = (bf16[512,2048]{1,0:T(8,128)(2,1)}, bf16[512,2048]{1,0:T(8,128)(2,1)}, f32[80,2048]{1,0:T(8,128)}) custom-call(bf16[512,2048]{1,0:T(8,128)(2,1)} %fresh_hbm.1, bf16[512,2048]{1,0:T(8,128)(2,1)} %older_hbm.1, bf16[512,2048]{1,0:T(8,128)(2,1)} %cot_hbm.1, bf16[40,2048]{1,0:T(8,128)(2,1)} %bitcast.3, bf16[40,2048]{1,0:T(8,128)(2,1)} %down_ref.1), custom_call_target="tpu_custom_call" | custom-call | tf_op jit(solution)/shard_map/pallas_call | solution.py:375
  82.5 2.0 %fusion = (f32[40,2048]{1,0:T(8,128)}, f32[2048,40]{0,1:T(8,128)}) fusion(f32[80,2048]{1,0:T(8,128)} %get-tuple-element.9), kind=kLoop, calls=%fused_computation.1 | loop fusion | bytes 1310720 | tf_op jit(solution)/shard_map/slice | solution.py:413
  84.5 0.0 copy-start
  84.5 3.3 %copy.11 = bf16[512,2048]{1,0:T(8,128)(2,1)} copy(bf16[512,2048]{1,0:T(8,128)(2,1)} %get-tuple-element.16) | data formatting | bytes 4194304
  87.8 0.0 copy-done
  87.8 1.3 %copy.12 = bf16[512,2048]{1,0:T(8,128)(2,1)} copy(bf16[512,2048]{1,0:T(8,128)(2,1)S(1)} %copy-done) | data formatting | bytes 4194304
Async XLA Ops:
  84.5 3.3 %copy-start = (bf16[512,2048]{1,0:T(8,128)(2,1)S(1)}, bf16[512,2048]{1,0:T(8,128)(2,1)}, u32[]{:S(2)}) copy-start(bf16[512,2048]{1,0:T(8,128)(2,1)} %get-tuple-element.17) | copy-start | bytes 6291460
where the time goes:
time: 89.2 us; the launch traced here: 89.1 us
  Pallas kernels  81.9 us (92%)
  local copies, waits for them, and re-layouts  6.59 us (7%)
    pallas_call x1, Pallas kernels, per_device(): pl.pallas_call(kernel, out_shape=(jax.ShapeDtypeStruct((rows, width), bf1...  81.9 us
    unnamed x4, local copies, waits for them, and re-layouts  4.63 us
    slice x1, local copies, waits for them, and re-layouts, per_device(): return (out, igrad, grads[:units].T, grads[units:])  1.96 us

commit v1 on v0

v1 whole, which is shorter than its diff:
```python
import jax
import jax.numpy as jnp
from jax import lax
from jax.experimental import pallas as pl
from jax.experimental.pallas import tpu as pltpu
from jax.sharding import PartitionSpec as P

MESH = pl.DeviceIdType.MESH
WINDOW = 8
REACH = WINDOW // 2
SLOTS = 2 * REACH + 1
SEAM = 32
COL_TILE = 512
CHUNKS = 4


def contract(left, right, dims):
    return lax.dot_general(left, right, (dims, ((), ())), preferred_element_type=jnp.float32)


def kernel(
    fresh_hbm, older_hbm, cot_hbm, up_hbm, down_hbm,
    out_hbm, igrad_hbm, gup_hbm, gdown_hbm,
    w, fresh, older, cot, up_v, down_v, grads_acc, act_t, gact_t, out_v, igrad_v, grads_v,
    sib_out, sib_in, x_out, x_in, x0_out, x0_in, z_out, z_in, z0_in, far_out, far_in,
    in_sem, out_sem,
    b_ss, b_rs, f_ss, f_rs, bs_ss, bs_rs, fs_ss, fs_rs,
    g_ss, g_rs, x0_ss, x0_rs,
    x_ss, x_rs, z_ss, z_rs, d_ss, d_rs, far_ss, far_rs,
):
    units, width = up_v.shape
    packed = 2 * units
    pair = 2 * packed
    half = width // 2
    chunk = half // CHUNKS
    rows = older.shape[0]
    count = lax.axis_size("blk")
    me = lax.axis_index("blk")
    g = lax.axis_index("dp")
    k = lax.rem(me, 2)
    chip = me // 2
    ahead = lax.rem(me + 2, count)
    behind = lax.rem(me + count - 2, count)
    sibling = me + 1 - 2 * k
    across = lax.rem(me + count + 2 * k - 1, count)
    other = 1 - g
    seam_up = lax.rem(chip, SEAM) == SEAM - 1
    seam_down = lax.rem(chip, SEAM) == 0

    barrier = pltpu.get_barrier_semaphore()
    peers = (
        (ahead, g), (behind, g), (sibling, g), (me, other),
        (ahead, other), (behind, other), (across, g), (across, other),
    )
    for peer in peers:
        pl.semaphore_signal(barrier, inc=1, device_id=peer, device_id_type=MESH)

    loads = [
        pltpu.make_async_copy(src, dst, in_sem.at[i])
        for i, (src, dst) in enumerate((
            (up_hbm, up_v), (down_hbm, down_v), (older_hbm, older), (cot_hbm, cot), (fresh_hbm, fresh),
        ))
    ]
    for load in loads:
        load.start()

    my_rows = pl.multiple_of(k * packed, 16)
    sib_rows = pl.multiple_of((1 - k) * packed, 16)
    my_cols = pl.multiple_of(g * half, 128)
    other_cols = pl.multiple_of(other * half, 128)
    nothing = jnp.zeros((packed, width), w.dtype)
    w[0, 0:packed, :] = nothing
    w[SLOTS - 1, packed:pair, :] = nothing

    @pl.when(k == 1)
    def _():
        w[0, packed:pair, :] = nothing

    @pl.when(k == 0)
    def _():
        w[SLOTS - 1, 0:packed, :] = nothing
        gact_t[REACH] = jnp.zeros((pair, rows), jnp.bfloat16)

    loads[0].wait()
    loads[1].wait()
    w[REACH, pl.ds(my_rows, packed), :] = jnp.concatenate([up_v[...], down_v[...]], axis=0)

    pl.semaphore_wait(barrier, len(peers))

    def remote(src, dst, send, recv, device):
        return pltpu.make_async_remote_copy(
            src_ref=src, dst_ref=dst, send_sem=send, recv_sem=recv,
            device_id=device, device_id_type=MESH,
        )

    def piece(slot, start, q):
        return w.at[slot, pl.ds(start, packed), pl.ds(q * half, half)]

    def send_back(h, q, device=behind):
        group = jnp.where(seam_down, other, g) if q == 1 else g
        return remote(
            piece(REACH + h, my_rows, q), piece(REACH + h + 1, my_rows, q),
            b_ss.at[h, q], b_rs.at[h + 1, q], (device, group),
        )

    def send_forth(h, q, device=ahead):
        group = jnp.where(seam_up, other, g) if q == 1 else g
        return remote(
            piece(REACH - h, my_rows, q), piece(REACH - h - 1, my_rows, q),
            f_ss.at[h, q], f_rs.at[h + 1, q], (device, group),
        )

    def recv_back(h, q, start=my_rows):
        dst = piece(REACH + h, start, q)
        return remote(dst, dst, b_ss.at[h, q], b_rs.at[h, q], (behind, g))

    def recv_forth(h, q, start=my_rows):
        dst = piece(REACH - h, start, q)
        return remote(dst, dst, f_ss.at[h, q], f_rs.at[h, q], (ahead, g))

    def share(slot, h, q, start, send, recv):
        ref = piece(slot, start, q)
        return remote(ref, ref, send.at[h, q], recv.at[h, q], (sibling, g))

    def share_back(h, q, start=my_rows):
        return share(REACH + h, h, q, start, bs_ss, bs_rs)

    def share_forth(h, q, start=my_rows):
        return share(REACH - h, h, q, start, fs_ss, fs_rs)

    def share_grads(h):
        return remote(sib_out.at[h], sib_in.at[h], g_ss.at[h], g_rs.at[h], (sibling, g))

    def swap(h, c):
        return remote(x_out.at[h, c], x_in.at[h, c], x_ss.at[h, c], x_rs.at[h, c], (me, other))

    def swap_last():
        return remote(x0_out, x0_in, x0_ss.at[0], x0_rs.at[0], (me, other))

    def carry(h, c):
        return remote(z_out.at[h, c], z_in.at[h - 1, c], z_ss.at[h, c], z_rs.at[h - 1, c], (ahead, g))

    def carry_last(c, part, cross):
        return remote(
            z_out.at[1, c], z0_in.at[part, c],
            (d_ss if cross else z_ss).at[1, c], (d_rs if cross else z_rs).at[0, c],
            (ahead, other if cross else g),
        )

    def far(c, cross):
        n = 1 if cross else 0
        return remote(
            far_out.at[n, c], far_in.at[n, c], far_ss.at[n, c], far_rs.at[n, c],
            (across, other if cross else g),
        )

    for q in range(2):
        send_back(0, q).start()
    for q in range(2):
        share_back(0, q).start()
        send_forth(0, q).start()

    def valid(offset):
        return jnp.logical_and(offset >= 0, offset < WINDOW)

    blank = jnp.zeros((units, rows), jnp.float32)

    def backward_acts(pre, through, keep):
        relu = jnp.maximum(pre, 0.0)
        gact = jnp.where(keep, through * 2.0 * relu, 0.0)
        return [gact, blank], [blank, jnp.where(keep, jnp.square(relu), 0.0)]

    def pack(parts):
        return jnp.concatenate(parts, axis=0).astype(jnp.bfloat16)

    def column_tile(t):
        return pl.ds(pl.multiple_of(t * COL_TILE, COL_TILE), COL_TILE)

    def compute_back(h):
        block = w[REACH + h]
        pre = contract(block, older[...], ((1,), (1,)))
        through = contract(block, cot[...], ((1,), (1,)))
        gact, act = [], []
        for p in range(2):
            first = p * packed
            one, two = backward_acts(
                pre[first:first + units], through[first + units:first + packed], valid(2 * h + p - k)
            )
            gact += one
            act += two
        gact_t[h] = pack(gact)
        act = pack(act)

        @pl.loop(0, width // COL_TILE)
        def _(t):
            cols = column_tile(t)
            grads_acc[h, :, cols] = (
                contract(gact_t[h], older[:, cols], ((1,), (0,)))
                + contract(act, cot[:, cols], ((1,), (0,)))
            )

        sib_out[h] = grads_acc[h, pl.ds(sib_rows, packed), :].astype(jnp.bfloat16)
        share_grads(h).start()

    def compute_far():
        block = w[SLOTS - 1, 0:packed, :]
        pre = contract(block, older[...], ((1,), (1,)))
        through = contract(block, cot[...], ((1,), (1,)))
        gact, act = backward_acts(pre[0:units], through[units:packed], True)
        gact, act = pack(gact), pack(act)
        gact_t[REACH] = jnp.concatenate([gact, jnp.zeros((packed, rows), jnp.bfloat16)], axis=0)
        for n in (1, 0):
            @pl.loop(0, half // COL_TILE)
            def _(t):
                cols = pl.ds(
                    pl.multiple_of((other_cols if n == 1 else my_cols) + t * COL_TILE, COL_TILE), COL_TILE
                )
                sums = (
                    contract(gact, older[:, cols], ((1,), (0,)))
                    + contract(act, cot[:, cols], ((1,), (0,)))
                ).astype(jnp.bfloat16)
                per = COL_TILE // chunk
                for i in range(per):
                    far_out[n, t * per + i] = sums[:, i * chunk:(i + 1) * chunk]
                    far(t * per + i, n == 1).start()

    def compute_forth(s):
        pre = contract(w[s], fresh[...], ((1,), (1,)))
        act = []
        for p in range(2):
            keep = valid(k - 2 * (s - REACH) - p)
            relu = jnp.maximum(pre[p * packed:p * packed + units], 0.0)
            act += [blank, jnp.where(keep, jnp.square(relu), 0.0)]
        act_t[s] = pack(act)

    def chunk_cols(start, c):
        return pl.ds(pl.multiple_of(start + c * chunk, chunk), chunk)

    def reduce_near(h):
        share_grads(h).wait_recv()

        @pl.loop(0, CHUNKS)
        def _(c):
            cols = chunk_cols(other_cols, c)
            x_out[h, c] = (
                grads_acc[h, pl.ds(my_rows, packed), cols] + sib_in[h, :, cols].astype(jnp.float32)
            ).astype(jnp.bfloat16)
            swap(h, c).start()

    def reduce_own():
        share_grads(0).wait_recv()
        x0_out[...] = (
            grads_acc[0, pl.ds(my_rows, packed), :] + sib_in[0].astype(jnp.float32)
        ).astype(jnp.bfloat16)
        swap_last().start()

    @pl.loop(0, REACH)
    def _(h):
        @pl.when(h == 0)
        def _():
            loads[2].wait()
            loads[3].wait()

        @pl.when(h > 0)
        def _():
            for q in range(2):
                recv_back(h, q).wait_recv()

                @pl.when(h + 1 < REACH)
                def _():
                    send_back(h, q).start()

                @pl.when(jnp.logical_and(h + 1 == REACH, k == 0))
                def _():
                    send_back(h, q, across).start()

                share_back(h, q).start()

                recv_forth(h, q).wait_recv()

                @pl.when(h + 1 < REACH)
                def _():
                    send_forth(h, q).start()

                @pl.when(jnp.logical_and(h + 1 == REACH, k == 1))
                def _():
                    send_forth(h, q, across).start()

                share_forth(h, q).start()

        @pl.when(h == 1)
        def _():
            reduce_own()

        @pl.when(h > 1)
        def _():
            reduce_near(h - 1)

        for q in range(2):
            share_back(h, q, sib_rows).wait_recv()
        compute_back(h)

        @pl.when(h == 0)
        def _():
            loads[4].wait()

        @pl.when(h > 0)
        def _():
            for q in range(2):
                share_forth(h, q, sib_rows).wait_recv()

        compute_forth(REACH - h)

    def chain(h, first):
        @pl.loop(0, CHUNKS)
        def _(c):
            cols = chunk_cols(my_cols, c)
            swap(h, c).wait_recv()
            total = (
                grads_acc[h, pl.ds(my_rows, packed), cols]
                + sib_in[h, :, cols].astype(jnp.float32)
                + x_in[h, c].astype(jnp.float32)
            )
            if not first:
                if h == REACH - 1:
                    far(c, True).wait_recv()
                    far(c, False).wait_recv()
                    total = total + far_in[0, c].astype(jnp.float32) + far_in[1, c].astype(jnp.float32)
                else:
                    carry(h + 1, c).wait_recv()
                    total = total + z_in[h, c].astype(jnp.float32)
            z_out[h, c] = total.astype(jnp.bfloat16)
            if h == 1:
                carry_last(c, g, False).start()
                carry_last(c, g, True).start()
            else:
                carry(h, c).start()

    def out_tiles(first, last):
        @pl.loop(first, last)
        def _(t):
            cols = column_tile(t)
            left = act_t[...].reshape((REACH + 1) * pair, rows)
            right = w[0:REACH + 1, :, cols].reshape((REACH + 1) * pair, COL_TILE)
            out_v[:, cols] = contract(left, right, ((0,), (0,))).astype(out_v.dtype)

    def igrad_tiles(first, last):
        @pl.loop(first, last)
        def _(t):
            cols = column_tile(t)
            left = gact_t[...].reshape((REACH + 1) * pair, rows)
            right = w[REACH:SLOTS, :, cols].reshape((REACH + 1) * pair, COL_TILE)
            igrad_v[:, cols] = contract(left, right, ((0,), (0,))).astype(igrad_v.dtype)

    reduce_near(REACH - 1)

    @pl.when(k == 1)
    def _():
        for q in range(2):
            recv_back(REACH, q, 0).wait_recv()
        compute_far()
        chain(REACH - 1, True)

    @pl.when(k == 0)
    def _():
        for q in range(2):
            recv_forth(REACH, q, packed).wait_recv()

    compute_forth(0)
    tiles = width // COL_TILE
    out_tiles(0, tiles)
    out_done = pltpu.make_async_copy(out_v, out_hbm, out_sem.at[0])
    out_done.start()

    @pl.when(k == 0)
    def _():
        chain(REACH - 1, False)

    igrad_tiles(0, tiles // 2)
    chain(2, False)
    igrad_tiles(tiles // 2, tiles)
    igrad_done = pltpu.make_async_copy(igrad_v, igrad_hbm, out_sem.at[1])
    igrad_done.start()
    chain(1, False)

    swap_last().wait_recv()
    for n in range(2):
        @pl.loop(0, CHUNKS)
        def _(c):
            part = other if n == 1 else g
            carry_last(c, part, n == 1).wait_recv()
            cols = chunk_cols(other_cols if n == 1 else my_cols, c)
            total = x0_out[:, cols].astype(jnp.float32) + x0_in[:, cols].astype(jnp.float32)
            grads_v[:, cols] = (total + z0_in[part, c].astype(jnp.float32)) * (1.0 / rows)

    last = [
        pltpu.make_async_copy(grads_v.at[0:units], gup_hbm, out_sem.at[2]),
        pltpu.make_async_copy(grads_v.at[units:packed], gdown_hbm, out_sem.at[3]),
    ]
    for copy in last:
        copy.start()

    @pl.loop(0, REACH)
    def _(h):
        share_grads(h).wait_send()
        for q in range(2):
            share_back(h, q).wait_send()

            @pl.when(jnp.logical_or(h + 1 < REACH, k == 0))
            def _():
                send_back(h, q).wait_send()

            @pl.when(jnp.logical_or(h + 1 < REACH, k == 1))
            def _():
                send_forth(h, q).wait_send()

            @pl.when(h > 0)
            def _():
                share_forth(h, q).wait_send()

    swap_last().wait_send()

    @pl.loop(0, CHUNKS)
    def _(c):
        carry_last(c, g, False).wait_send()
        carry_last(c, g, True).wait_send()
        for h in range(1, REACH):
            swap(h, c).wait_send()
        for h in range(2, REACH):
            carry(h, c).wait_send()

        @pl.when(k == 1)
        def _():
            far(c, False).wait_send()
            far(c, True).wait_send()

    out_done.wait()
    igrad_done.wait()
    for copy in last:
        copy.wait()


def per_device(fresh_rows, older_rows, older_cotangent, weight_up, weight_down):
    rows, width = fresh_rows.shape
    units = weight_up.shape[1]
    packed = 2 * units
    pair = 2 * packed
    chunk = width // 2 // CHUNKS
    bf16, f32 = jnp.bfloat16, jnp.float32
    dma = pltpu.SemaphoreType.DMA
    out, igrad, grad_up, grad_down = pl.pallas_call(
        kernel,
        out_shape=(
            jax.ShapeDtypeStruct((rows, width), bf16),
            jax.ShapeDtypeStruct((rows, width), bf16),
            jax.ShapeDtypeStruct((units, width), f32),
            jax.ShapeDtypeStruct((units, width), f32),
        ),
        in_specs=[pl.BlockSpec(memory_space=pl.ANY)] * 5,
        out_specs=[pl.BlockSpec(memory_space=pl.ANY)] * 4,
        scratch_shapes=[
            pltpu.VMEM((SLOTS, pair, width), bf16),
            pltpu.VMEM((rows, width), bf16),
            pltpu.VMEM((rows, width), bf16),
            pltpu.VMEM((rows, width), bf16),
            pltpu.VMEM((units, width), bf16),
            pltpu.VMEM((units, width), bf16),
            pltpu.VMEM((REACH, pair, width), f32),
            pltpu.VMEM((REACH + 1, pair, rows), bf16),
            pltpu.VMEM((REACH + 1, pair, rows), bf16),
            pltpu.VMEM((rows, width), bf16),
            pltpu.VMEM((rows, width), bf16),
            pltpu.VMEM((packed, width), f32),
            pltpu.VMEM((REACH, packed, width), bf16),
            pltpu.VMEM((REACH, packed, width), bf16),
            pltpu.VMEM((REACH, CHUNKS, packed, chunk), bf16),
            pltpu.VMEM((REACH, CHUNKS, packed, chunk), bf16),
            pltpu.VMEM((packed, width), bf16),
            pltpu.VMEM((packed, width), bf16),
            pltpu.VMEM((REACH, CHUNKS, packed, chunk), bf16),
            pltpu.VMEM((REACH, CHUNKS, packed, chunk), bf16),
            pltpu.VMEM((2, CHUNKS, packed, chunk), bf16),
            pltpu.VMEM((2, CHUNKS, packed, chunk), bf16),
            pltpu.VMEM((2, CHUNKS, packed, chunk), bf16),
            dma((5,)), dma((4,)),
        ]
        + [dma((REACH + 1, 2))] * 8
        + [dma((REACH,))] * 2
        + [dma((1,))] * 2
        + [dma((REACH, CHUNKS))] * 2
        + [dma((REACH, CHUNKS))] * 2
        + [dma((REACH, CHUNKS))] * 2
        + [dma((2, CHUNKS))] * 2,
        compiler_params=pltpu.CompilerParams(
            collective_id=0, has_side_effects=True, vmem_limit_bytes=56 * 2**20
        ),
    )(fresh_rows, older_rows, older_cotangent, weight_up.T, weight_down)
    return out, igrad, grad_up.T, grad_down


def solution(mesh):
    in_specs = (
        P(("blk", "dp"), None),
        P(("blk", "dp"), None),
        P(("blk", "dp"), None),
        P(None, "blk"),
        P("blk", None),
    )
    out_specs = (P(("blk", "dp"), None), P(("blk", "dp"), None), P(None, "blk"), P("blk", None))
    return jax.shard_map(
        per_device, mesh=mesh, in_specs=in_specs, out_specs=out_specs, check_vma=False
    )
```

time: 89.2 us -> 82.3 us (0.923)
  the two profiles are of different devices: /device:TPU:96 before, /device:TPU:33 now
where the time goes in v1:
time: 82.3 us; the launch traced here: 82.2 us
  Pallas kernels  75.4 us (92%)
  local copies, waits for them, and re-layouts  6.09 us (7%)
    pallas_call x1, Pallas kernels, per_device(): pl.pallas_call(kernel, out_shape=(jax.ShapeDtypeStruct((rows, width), bf1...  75.4 us
    unnamed x10, local copies, waits for them, and re-layouts  6.09 us

profile of v1, /device:TPU:33, one launch (start us, length us, event | category | flops | bytes accessed | tf_op | source)
XLA Modules:
  0.0 82.2 jit_solution(12977849858836599391)
XLA Ops:
  0.6 75.4 %shard_map.84 = (bf16[512,2048]{1,0:T(8,128)(2,1)}, bf16[512,2048]{1,0:T(8,128)(2,1)}, f32[40,2048]{1,0:T(8,128)}, f32[40,2048]{1,0:T(8,128)}) custom-call(bf16[512,2048]{1,0:T(8,128)(2,1)} %fresh_hbm.1, bf16[512,2048]{1,0:T(8,128)(2,1)} %older_hbm.1, bf16[512,2048]{1,0:T(8,128)(2,1)} %cot_hbm.1, bf16[40,2048]{1,0:T(8,128)(2,1)} %bitcast.3, ...), custom_call_target="tpu_custom_call" | custom-call | tf_op jit(solution)/shard_map/pallas_call | solution.py:451
  76.1 0.0 copy-start
  76.1 3.3 %copy.13 = bf16[512,2048]{1,0:T(8,128)(2,1)} copy(bf16[512,2048]{1,0:T(8,128)(2,1)} %get-tuple-element.16) | data formatting | bytes 4194304
  79.4 0.0 copy-done
  79.4 0.0 copy-start.2
  79.4 0.0 copy-start.1
  79.4 1.3 %copy.14 = bf16[512,2048]{1,0:T(8,128)(2,1)} copy(bf16[512,2048]{1,0:T(8,128)(2,1)S(1)} %copy-done) | data formatting | bytes 4194304
  80.7 0.0 copy-done.2
  80.7 0.7 copy.15
  81.5 0.0 copy-done.1
  81.5 0.7 copy.16
Async XLA Ops:
  76.1 3.3 %copy-start = (bf16[512,2048]{1,0:T(8,128)(2,1)S(1)}, bf16[512,2048]{1,0:T(8,128)(2,1)}, u32[]{:S(2)}) copy-start(bf16[512,2048]{1,0:T(8,128)(2,1)} %get-tuple-element.17) | copy-start | bytes 6291460
  79.4 1.3 %copy-start.2 = (f32[40,2048]{1,0:T(8,128)S(1)}, f32[40,2048]{1,0:T(8,128)}, u32[]{:S(2)}) copy-start(f32[40,2048]{1,0:T(8,128)} %get-tuple-element.10) | copy-start | bytes 983044
  79.4 2.1 %copy-start.1 = (f32[40,2048]{1,0:T(8,128)S(1)}, f32[40,2048]{1,0:T(8,128)}, u32[]{:S(2)}) copy-start(f32[40,2048]{1,0:T(8,128)} %get-tuple-element.19) | copy-start | bytes 983044

commit v2 on v1

--- a/solution.py
+++ b/solution.py
@@ -20,10 +20,10 @@
 
 def kernel(
     fresh_hbm, older_hbm, cot_hbm, up_hbm, down_hbm,
-    out_hbm, igrad_hbm, gup_hbm, gdown_hbm,
-    w, fresh, older, cot, up_v, down_v, grads_acc, act_t, gact_t, out_v, igrad_v, grads_v,
+    out_v, igrad_v, gup_v, gdown_v,
+    w, fresh, older, cot, up_v, down_v, grads_acc, act_t, gact_t,
     sib_out, sib_in, x_out, x_in, x0_out, x0_in, z_out, z_in, z0_in, far_out, far_in,
-    in_sem, out_sem,
+    in_sem,
     b_ss, b_rs, f_ss, f_rs, bs_ss, bs_rs, fs_ss, fs_rs,
     g_ss, g_rs, x0_ss, x0_rs,
     x_ss, x_rs, z_ss, z_rs, d_ss, d_rs, far_ss, far_rs,
@@ -254,52 +254,47 @@
         ).astype(jnp.bfloat16)
         swap_last().start()
 
+    def pass_on(h, q):
+        recv_back(h, q).wait_recv()
+
+        @pl.when(h + 1 < REACH)
+        def _():
+            send_back(h, q).start()
+
+        @pl.when(jnp.logical_and(h + 1 == REACH, k == 0))
+        def _():
+            send_back(h, q, across).start()
+
+        share_back(h, q).start()
+        recv_forth(h, q).wait_recv()
+
+        @pl.when(h + 1 < REACH)
+        def _():
+            send_forth(h, q).start()
+
+        @pl.when(jnp.logical_and(h + 1 == REACH, k == 1))
+        def _():
+            send_forth(h, q, across).start()
+
+        share_forth(h, q).start()
+
+    loads[2].wait()
+    loads[3].wait()
+
     @pl.loop(0, REACH)
     def _(h):
-        @pl.when(h == 0)
-        def _():
-            loads[2].wait()
-            loads[3].wait()
-
         @pl.when(h > 0)
         def _():
-            for q in range(2):
-                recv_back(h, q).wait_recv()
-
-                @pl.when(h + 1 < REACH)
-                def _():
-                    send_back(h, q).start()
-
-                @pl.when(jnp.logical_and(h + 1 == REACH, k == 0))
-                def _():
-                    send_back(h, q, across).start()
-
-                share_back(h, q).start()
-
-                recv_forth(h, q).wait_recv()
-
-                @pl.when(h + 1 < REACH)
-                def _():
-                    send_forth(h, q).start()
-
-                @pl.when(jnp.logical_and(h + 1 == REACH, k == 1))
-                def _():
-                    send_forth(h, q, across).start()
-
-                share_forth(h, q).start()
-
-        @pl.when(h == 1)
-        def _():
-            reduce_own()
-
-        @pl.when(h > 1)
-        def _():
-            reduce_near(h - 1)
+            pass_on(h, 1)
 
         for q in range(2):
             share_back(h, q, sib_rows).wait_recv()
         compute_back(h)
 
+        @pl.when(h + 1 < REACH)
+        def _():
+            pass_on(h + 1, 0)
+
         @pl.when(h == 0)
         def _():
             loads[4].wait()
@@ -310,6 +305,14 @@
                 share_forth(h, q, sib_rows).wait_recv()
 
         compute_forth(REACH - h)
+
+        @pl.when(h == 0)
+        def _():
+            reduce_own()
+
+        @pl.when(h > 0)
+        def _():
+            reduce_near(h)
 
     def chain(h, first):
         @pl.loop(0, CHUNKS)
@@ -352,8 +355,6 @@
             right = w[REACH:SLOTS, :, cols].reshape((REACH + 1) * pair, COL_TILE)
             igrad_v[:, cols] = contract(left, right, ((0,), (0,))).astype(igrad_v.dtype)
 
-    reduce_near(REACH - 1)
-
     @pl.when(k == 1)
     def _():
         for q in range(2):
@@ -369,8 +370,6 @@
     compute_forth(0)
     tiles = width // COL_TILE
     out_tiles(0, tiles)
-    out_done = pltpu.make_async_copy(out_v, out_hbm, out_sem.at[0])
-    out_done.start()
 
     @pl.when(k == 0)
     def _():
@@ -379,8 +378,6 @@
     igrad_tiles(0, tiles // 2)
     chain(2, False)
     igrad_tiles(tiles // 2, tiles)
-    igrad_done = pltpu.make_async_copy(igrad_v, igrad_hbm, out_sem.at[1])
-    igrad_done.start()
     chain(1, False)
 
     swap_last().wait_recv()
@@ -391,14 +388,9 @@
             carry_last(c, part, n == 1).wait_recv()
             cols = chunk_cols(other_cols if n == 1 else my_cols, c)
             total = x0_out[:, cols].astype(jnp.float32) + x0_in[:, cols].astype(jnp.float32)
-            grads_v[:, cols] = (total + z0_in[part, c].astype(jnp.float32)) * (1.0 / rows)
-
-    last = [
-        pltpu.make_async_copy(grads_v.at[0:units], gup_hbm, out_sem.at[2]),
-        pltpu.make_async_copy(grads_v.at[units:packed], gdown_hbm, out_sem.at[3]),
-    ]
-    for copy in last:
-        copy.start()
+            total = (total + z0_in[part, c].astype(jnp.float32)) * (1.0 / rows)
+            gup_v[:, cols] = total[0:units]
+            gdown_v[:, cols] = total[units:packed]
 
     @pl.loop(0, REACH)
     def _(h):
@@ -433,11 +425,6 @@
         def _():
             far(c, False).wait_send()
             far(c, True).wait_send()
-
-    out_done.wait()
-    igrad_done.wait()
-    for copy in last:
-        copy.wait()
 
 
 def per_device(fresh_rows, older_rows, older_cotangent, weight_up, weight_down):
@@ -451,13 +438,13 @@
     out, igrad, grad_up, grad_down = pl.pallas_call(
         kernel,
         out_shape=(
-            jax.ShapeDtypeStruct((rows, width), bf16),
-            jax.ShapeDtypeStruct((rows, width), bf16),
-            jax.ShapeDtypeStruct((units, width), f32),
-            jax.ShapeDtypeStruct((units, width), f32),
+            pltpu.VMEM((rows, width), bf16),
+            pltpu.VMEM((rows, width), bf16),
+            pltpu.VMEM((units, width), f32),
+            pltpu.VMEM((units, width), f32),
         ),
         in_specs=[pl.BlockSpec(memory_space=pl.ANY)] * 5,
-        out_specs=[pl.BlockSpec(memory_space=pl.ANY)] * 4,
+        out_specs=[pl.BlockSpec(memory_space=pltpu.VMEM)] * 4,
         scratch_shapes=[
             pltpu.VMEM((SLOTS, pair, width), bf16),
             pltpu.VMEM((rows, width), bf16),
@@ -468,9 +455,6 @@
             pltpu.VMEM((REACH, pair, width), f32),
             pltpu.VMEM((REACH + 1, pair, rows), bf16),
             pltpu.VMEM((REACH + 1, pair, rows), bf16),
-            pltpu.VMEM((rows, width), bf16),
-            pltpu.VMEM((rows, width), bf16),
-            pltpu.VMEM((packed, width), f32),
             pltpu.VMEM((REACH, packed, width), bf16),
             pltpu.VMEM((REACH, packed, width), bf16),
             pltpu.VMEM((REACH, CHUNKS, packed, chunk), bf16),
@@ -482,7 +466,7 @@
             pltpu.VMEM((2, CHUNKS, packed, chunk), bf16),
             pltpu.VMEM((2, CHUNKS, packed, chunk), bf16),
             pltpu.VMEM((2, CHUNKS, packed, chunk), bf16),
-            dma((5,)), dma((4,)),
+            dma((5,)),
         ]
         + [dma((REACH + 1, 2))] * 8
         + [dma((REACH,))] * 2

time: 82.3 us -> 79.6 us (0.967)
  local copies, waits for them, and re-layouts: 6.09 us -> 4.09 us
    unnamed x10 -> x4, local copies, waits for them, and re-layouts: 6.09 us -> 4.09 us
where the time goes in v2:
time: 79.6 us; the launch traced here: 79.5 us
  Pallas kernels  74.8 us (94%)
  local copies, waits for them, and re-layouts  4.09 us (5%)
    pallas_call x1, Pallas kernels, per_device(): pl.pallas_call(kernel, out_shape=(pltpu.VMEM((rows, width), bf16), pltpu....  74.8 us
    unnamed x4, local copies, waits for them, and re-layouts  4.09 us

profile of v2, /device:TPU:33, one launch (start us, length us, event | category | flops | bytes accessed | tf_op | source)
XLA Modules:
  0.0 79.5 jit_solution(13173674021013013799)
XLA Ops:
  0.6 74.8 %shard_map.84 = (bf16[512,2048]{1,0:T(8,128)(2,1)S(1)}, bf16[512,2048]{1,0:T(8,128)(2,1)S(1)}, f32[40,2048]{1,0:T(8,128)S(1)}, f32[40,2048]{1,0:T(8,128)S(1)}) custom-call(bf16[512,2048]{1,0:T(8,128)(2,1)} %fresh_hbm.1, bf16[512,2048]{1,0:T(8,128)(2,1)} %older_hbm.1, bf16[512,2048]{1,0:T(8,128)(2,1)} %cot_hbm.1, bf16[40,2048]{1,0:T(8,128)(2,1)} %bitcast.3, ...), custom_call_target="tpu_custom_call" | custom-call | tf_op jit(solution)/shard_map/pallas_call | solution.py:438
  75.4 1.3 %copy.13 = bf16[512,2048]{1,0:T(8,128)(2,1)} copy(bf16[512,2048]{1,0:T(8,128)(2,1)S(1)} %get-tuple-element.12) | data formatting | bytes 4194304
  76.8 0.7 copy.15
  77.5 0.7 copy.16
  78.2 1.3 %copy.14 = bf16[512,2048]{1,0:T(8,128)(2,1)} copy(bf16[512,2048]{1,0:T(8,128)(2,1)S(1)} %get-tuple-element.13) | data formatting | bytes 4194304

commit v3 on v2

--- a/solution.py
+++ b/solution.py
@@ -46,6 +46,7 @@
     other = 1 - g
     seam_up = lax.rem(chip, SEAM) == SEAM - 1
     seam_down = lax.rem(chip, SEAM) == 0
+    late = lax.rem(chip, SEAM) < REACH
 
     barrier = pltpu.get_barrier_semaphore()
     peers = (
@@ -254,7 +255,7 @@
         ).astype(jnp.bfloat16)
         swap_last().start()
 
-    def pass_on(h, q):
+    def pass_back(h, q):
         recv_back(h, q).wait_recv()
 
         @pl.when(h + 1 < REACH)
@@ -266,6 +267,8 @@
             send_back(h, q, across).start()
 
         share_back(h, q).start()
+
+    def pass_forth(h, q):
         recv_forth(h, q).wait_recv()
 
         @pl.when(h + 1 < REACH)
@@ -277,6 +280,10 @@
             send_forth(h, q, across).start()
 
         share_forth(h, q).start()
+
+    def forth_ready(h):
+        for q in range(2):
+            share_forth(h, q, sib_rows).wait_recv()
 
     loads[2].wait()
     loads[3].wait()
@@ -285,7 +292,11 @@
     def _(h):
         @pl.when(h > 0)
         def _():
-            pass_on(h, 1)
+            pass_back(h, 1)
+
+        @pl.when(jnp.logical_and(h > 0, jnp.logical_not(late)))
+        def _():
+            pass_forth(h, 1)
 
         for q in range(2):
             share_back(h, q, sib_rows).wait_recv()
@@ -293,26 +304,36 @@
 
         @pl.when(h + 1 < REACH)
         def _():
-            pass_on(h + 1, 0)
+            pass_back(h + 1, 0)
+
+        @pl.when(jnp.logical_and(h + 1 < REACH, jnp.logical_not(late)))
+        def _():
+            pass_forth(h + 1, 0)
+
+        @pl.when(jnp.logical_and(h > 0, late))
+        def _():
+            pass_forth(h, 1)
+
+        @pl.when(h == 1)
+        def _():
+            loads[4].wait()
+
+        @pl.when(h > 1)
+        def _():
+            forth_ready(h - 1)
+
+        @pl.when(h > 0)
+        def _():
+            compute_forth(REACH - h + 1)
+            reduce_near(h)
 
         @pl.when(h == 0)
         def _():
-            loads[4].wait()
-
-        @pl.when(h > 0)
-        def _():
-            for q in range(2):
-                share_forth(h, q, sib_rows).wait_recv()
-
-        compute_forth(REACH - h)
-
-        @pl.when(h == 0)
-        def _():
             reduce_own()
 
-        @pl.when(h > 0)
-        def _():
-            reduce_near(h)
+        @pl.when(jnp.logical_and(h + 1 < REACH, late))
+        def _():
+            pass_forth(h + 1, 0)
 
     def chain(h, first):
         @pl.loop(0, CHUNKS)
@@ -362,23 +383,30 @@
         compute_far()
         chain(REACH - 1, True)
 
+    tiles = width // COL_TILE
+
+    @pl.when(k == 0)
+    def _():
+        igrad_tiles(0, tiles)
+        chain(REACH - 1, False)
+
+    chain(2, False)
+
+    @pl.when(k == 1)
+    def _():
+        igrad_tiles(0, tiles)
+
+    forth_ready(REACH - 1)
+    compute_forth(1)
+    chain(1, False)
+
     @pl.when(k == 0)
     def _():
         for q in range(2):
             recv_forth(REACH, q, packed).wait_recv()
 
     compute_forth(0)
-    tiles = width // COL_TILE
     out_tiles(0, tiles)
-
-    @pl.when(k == 0)
-    def _():
-        chain(REACH - 1, False)
-
-    igrad_tiles(0, tiles // 2)
-    chain(2, False)
-    igrad_tiles(tiles // 2, tiles)
-    chain(1, False)
 
     swap_last().wait_recv()
     for n in range(2):

time: 79.6 us -> 75.9 us (0.954); the launches traced: 79.5 us -> 74.5 us
  Pallas kernels: 74.8 us -> 69.8 us
    pallas_call x1, Pallas kernels: 74.8 us -> 69.8 us  [per_device(): pl.pallas_call(kernel, out_shape=(pltpu.VMEM((rows, width), bf16), pltpu....]
where the time goes in v3:
time: 75.9 us; the launch traced here: 74.5 us
  Pallas kernels  69.8 us (92%)
  local copies, waits for them, and re-layouts  4.09 us (5%)
    pallas_call x1, Pallas kernels, per_device(): pl.pallas_call(kernel, out_shape=(pltpu.VMEM((rows, width), bf16), pltpu....  69.8 us
    unnamed x4, local copies, waits for them, and re-layouts  4.09 us

profile of v3, /device:TPU:33, one launch (start us, length us, event | category | flops | bytes accessed | tf_op | source)
XLA Modules:
  0.0 74.5 jit_solution(17339221758567148572)
XLA Ops:
  0.6 69.8 %shard_map.84 = (bf16[512,2048]{1,0:T(8,128)(2,1)S(1)}, bf16[512,2048]{1,0:T(8,128)(2,1)S(1)}, f32[40,2048]{1,0:T(8,128)S(1)}, f32[40,2048]{1,0:T(8,128)S(1)}) custom-call(bf16[512,2048]{1,0:T(8,128)(2,1)} %fresh_hbm.1, bf16[512,2048]{1,0:T(8,128)(2,1)} %older_hbm.1, bf16[512,2048]{1,0:T(8,128)(2,1)} %cot_hbm.1, bf16[40,2048]{1,0:T(8,128)(2,1)} %bitcast.3, ...), custom_call_target="tpu_custom_call" | custom-call | tf_op jit(solution)/shard_map/pallas_call | solution.py:466
  70.4 1.3 %copy.13 = bf16[512,2048]{1,0:T(8,128)(2,1)} copy(bf16[512,2048]{1,0:T(8,128)(2,1)S(1)} %get-tuple-element.12) | data formatting | bytes 4194304
  71.7 0.7 copy.15
  72.5 0.7 copy.16
  73.2 1.3 %copy.14 = bf16[512,2048]{1,0:T(8,128)(2,1)} copy(bf16[512,2048]{1,0:T(8,128)(2,1)S(1)} %get-tuple-element.13) | data formatting | bytes 4194304

commit v4 on v3

--- a/solution.py
+++ b/solution.py
@@ -105,7 +105,7 @@
         )
 
     def send_forth(h, q, device=ahead):
-        group = jnp.where(seam_up, other, g) if q == 1 else g
+        group = jnp.where(jnp.logical_and(seam_up, k == 1), other, g)
         return remote(
             piece(REACH - h, my_rows, q), piece(REACH - h - 1, my_rows, q),
             f_ss.at[h, q], f_rs.at[h + 1, q], (device, group),

time: 75.9 us -> 75.7 us (level)
  no operation moved by 1% of the time
where the time goes in v4:
time: 75.7 us; the launch traced here: 74.7 us
  Pallas kernels  70 us (92%)
  local copies, waits for them, and re-layouts  4.09 us (5%)
    pallas_call x1, Pallas kernels, per_device(): pl.pallas_call(kernel, out_shape=(pltpu.VMEM((rows, width), bf16), pltpu....  70 us
    unnamed x4, local copies, waits for them, and re-layouts  4.09 us

profile of v4, /device:TPU:33, one launch (start us, length us, event | category | flops | bytes accessed | tf_op | source)
XLA Modules:
  0.0 74.7 jit_solution(17430148347778398045)
XLA Ops:
  0.6 70.0 %shard_map.84 = (bf16[512,2048]{1,0:T(8,128)(2,1)S(1)}, bf16[512,2048]{1,0:T(8,128)(2,1)S(1)}, f32[40,2048]{1,0:T(8,128)S(1)}, f32[40,2048]{1,0:T(8,128)S(1)}) custom-call(bf16[512,2048]{1,0:T(8,128)(2,1)} %fresh_hbm.1, bf16[512,2048]{1,0:T(8,128)(2,1)} %older_hbm.1, bf16[512,2048]{1,0:T(8,128)(2,1)} %cot_hbm.1, bf16[40,2048]{1,0:T(8,128)(2,1)} %bitcast.3, ...), custom_call_target="tpu_custom_call" | custom-call | tf_op jit(solution)/shard_map/pallas_call | solution.py:466
  70.6 1.3 %copy.13 = bf16[512,2048]{1,0:T(8,128)(2,1)} copy(bf16[512,2048]{1,0:T(8,128)(2,1)S(1)} %get-tuple-element.12) | data formatting | bytes 4194304
  72.0 0.7 copy.15
  72.7 0.7 copy.16
  73.4 1.3 %copy.14 = bf16[512,2048]{1,0:T(8,128)(2,1)} copy(bf16[512,2048]{1,0:T(8,128)(2,1)S(1)} %get-tuple-element.13) | data formatting | bytes 4194304

commit v5 on v4

--- a/solution.py
+++ b/solution.py
@@ -76,6 +76,7 @@
     @pl.when(k == 1)
     def _():
         w[0, packed:pair, :] = nothing
+        act_t[0] = jnp.zeros((pair, rows), jnp.bfloat16)
 
     @pl.when(k == 0)
     def _():
@@ -404,8 +405,8 @@
     def _():
         for q in range(2):
             recv_forth(REACH, q, packed).wait_recv()
-
-    compute_forth(0)
+        compute_forth(0)
+
     out_tiles(0, tiles)
 
     swap_last().wait_recv()

time: 75.7 us -> 75.7 us (level)
  no operation moved by 1% of the time
where the time goes in v5:
time: 75.7 us; the launch traced here: 74.7 us
  Pallas kernels  70 us (92%)
  local copies, waits for them, and re-layouts  4.09 us (5%)
    pallas_call x1, Pallas kernels, per_device(): pl.pallas_call(kernel, out_shape=(pltpu.VMEM((rows, width), bf16), pltpu....  70 us
    unnamed x4, local copies, waits for them, and re-layouts  4.09 us

profile of v5, /device:TPU:33, one launch (start us, length us, event | category | flops | bytes accessed | tf_op | source)
XLA Modules:
  0.0 74.7 jit_solution(927035680336638884)
XLA Ops:
  0.6 70.0 %shard_map.84 = (bf16[512,2048]{1,0:T(8,128)(2,1)S(1)}, bf16[512,2048]{1,0:T(8,128)(2,1)S(1)}, f32[40,2048]{1,0:T(8,128)S(1)}, f32[40,2048]{1,0:T(8,128)S(1)}) custom-call(bf16[512,2048]{1,0:T(8,128)(2,1)} %fresh_hbm.1, bf16[512,2048]{1,0:T(8,128)(2,1)} %older_hbm.1, bf16[512,2048]{1,0:T(8,128)(2,1)} %cot_hbm.1, bf16[40,2048]{1,0:T(8,128)(2,1)} %bitcast.3, ...), custom_call_target="tpu_custom_call" | custom-call | tf_op jit(solution)/shard_map/pallas_call | solution.py:467
  70.6 1.3 %copy.13 = bf16[512,2048]{1,0:T(8,128)(2,1)} copy(bf16[512,2048]{1,0:T(8,128)(2,1)S(1)} %get-tuple-element.12) | data formatting | bytes 4194304
  72.0 0.7 copy.15
  72.7 0.7 copy.16
  73.4 1.3 %copy.14 = bf16[512,2048]{1,0:T(8,128)(2,1)} copy(bf16[512,2048]{1,0:T(8,128)(2,1)S(1)} %get-tuple-element.13) | data formatting | bytes 4194304
